TPU v7x, 256 devices: a whole 4x4x8 slice. The times are simulated.
256 devices in a mesh: dp: 16 (over y, z_lo), ctx: 16 (over x, z_hi, core).
Axes of the slice: x: 4, y: 4, z: 8 (z_hi: 2, z_lo: 4; z = z_hi * 4 + z_lo), core: 2. Of those that a mesh axis runs over, the one named last changes fastest.
Arguments:
- layer_inputs: bfloat16 [32768, 6144], P(('dp', 'ctx')), may hold values from -6 to 6
- queries: bfloat16 [32768, 6144], P(('dp', 'ctx')), may hold values from -128 to 128
- key_states: bfloat16 [32768, 512], P(('dp', 'ctx')), may hold values from -6 to 6
- value_states: bfloat16 [32768, 512], P(('dp', 'ctx')), may hold values from -6 to 6
- output_grad: bfloat16 [32768, 6144], P(('dp', 'ctx')), may hold values from -6 to 6
- short_segments: int32 [256, 64], P(('dp', 'ctx')), may hold values from 0 to 7, never falling along the last dimension, each value on 1 to 16 neighbouring positions
- master: float32 [16, 384, 512], P('ctx', 'dp'), may hold values from -0.078125 to 0.078125
- first_moment: float32 [16, 384, 512], P('ctx', 'dp'), may hold values from -0.015625 to 0.015625
- second_moment: float32 [16, 384, 512], P('ctx', 'dp'), may hold values from 1e-07 to 1e-05
Outputs:
- grad_queries: bfloat16 [32768, 6144], P(('dp', 'ctx'))
- grad_values: bfloat16 [32768, 512], P(('dp', 'ctx'))
- new_master: float32 [16, 384, 512], P('ctx', 'dp')
- new_first: float32 [16, 384, 512], P('ctx', 'dp')
- new_second: float32 [16, 384, 512], P('ctx', 'dp')
- new_weight: bfloat16 [16, 384, 512], P('ctx')
Inputs may be any that keep to these rules, and one draw needn't show every extreme that they name: `short_segments`: on each device the short tokens form 8 documents numbered in order, each of 1 to 16 tokens, one of exactly that length.
All inputs are finite; a program needn't handle non-finite values.
Results may differ from a plain program's by a relative error of at most 0.0074.
Values may be sent and summed in bfloat16 or wider, within the bound.
A program may use at most 128 MiB of HBM per device.

v0:
```python
import functools

import jax
import jax.numpy as jnp
from jax import lax
from jax.experimental import pallas as pl
from jax.experimental.pallas import tpu as pltpu
from jax.sharding import PartitionSpec as P

D = 6144
HEAD = 128
GROUPS = 12
HK = 4
SHORT_FIRST = 2
LONG_DEV = 64
SHORT_DEV = 64
TOK_DEV = 128
CHUNK = 128
KD = 512
QD = 6144
HALF_Q = 3072
HALF_K = 256
NY, NZL, NX, NZH, NC = 4, 4, 4, 2, 2
NZ = NZL * NZH

LEARN_RATE = 0.001
BETA_ONE = 0.9
BETA_TWO = 0.95
ADAM_EPS = 1e-08
DECAY = 0.1
STEP_COUNT = 10

MESH = pl.DeviceIdType.MESH
FACTOR = HEAD**-0.5
EXP_FACTOR = FACTOR * 1.4426950408889634
NEG = -1e30
BF = jnp.bfloat16
VMEM_LIMIT = 63 << 20
F32 = jnp.float32
NT = (((1,), (1,)), ((), ()))
TN = (((0,), (0,)), ((), ()))


def dot(a, b, dims=(((1,), (0,)), ((), ()))):
    return lax.dot_general(a, b, dims, preferred_element_type=F32)


def place():
    d = lax.axis_index("dp")
    c = lax.axis_index("ctx")
    return d // NZL, d % NZL, c // (NZH * NC), (c // NC) % NZH, c % NC


def device(y, z_lo, x, z_hi, core):
    return (y * NZL + z_lo, (x * NZH + z_hi) * NC + core)


def remote(src, dst, send, recv, peer):
    return pltpu.make_async_remote_copy(
        src_ref=src, dst_ref=dst, send_sem=send, recv_sem=recv, device_id=peer, device_id_type=MESH
    )


def lanes(start, size):
    return pl.ds(pl.multiple_of(start, 128), size)


def rows(start, size, unit):
    return pl.ds(pl.multiple_of(start, unit), size)


def short_mask(seg_ref):
    segment = seg_ref[...]
    square = jnp.broadcast_to(segment, (SHORT_DEV, SHORT_DEV))
    diag = lax.broadcasted_iota(jnp.int32, (SHORT_DEV, SHORT_DEV), 0) == lax.broadcasted_iota(
        jnp.int32, (SHORT_DEV, SHORT_DEV), 1
    )
    column = jnp.sum(jnp.where(diag, square.astype(F32), 0.0), axis=1, keepdims=True)
    row = jnp.concatenate([segment.astype(F32)] * 2, axis=1)
    key = lax.broadcasted_iota(jnp.int32, (SHORT_DEV, 128), 0)
    token = lax.broadcasted_iota(jnp.int32, (SHORT_DEV, 128), 1) % SHORT_DEV
    pair = jnp.where((column == row) & (key <= token), 0.0, NEG)
    return jnp.concatenate([pair] * (GROUPS // 2), axis=1)


def short_head(kh, bias, q_ref, g_ref, k_ref, v_ref, dq_ref, dk_ref, dv_ref):
    width = GROUPS * HEAD
    q = q_ref[:, lanes(kh * width, width)]
    g = g_ref[:, lanes(kh * width, width)]
    k = k_ref[:, lanes(kh * HEAD, HEAD)]
    v = v_ref[:, lanes(kh * HEAD, HEAD)]
    q = jnp.concatenate([q[:, i * HEAD : (i + 1) * HEAD] for i in range(GROUPS)], axis=0)
    g = jnp.concatenate([g[:, i * HEAD : (i + 1) * HEAD] for i in range(GROUPS)], axis=0)
    scores = dot(k, q, NT) + bias
    top = jnp.max(scores, axis=0, keepdims=True)
    raised = jnp.exp2((scores - top) * EXP_FACTOR)
    probs = raised * (1.0 / jnp.sum(raised, axis=0, keepdims=True))
    probs_low = probs.astype(BF)
    grad_probs = dot(v, g, NT)
    delta = jnp.sum(probs_low.astype(F32) * grad_probs, axis=0, keepdims=True)
    grad_scores = (probs * FACTOR * (grad_probs - delta)).astype(BF)
    dv_ref[:, lanes(kh * HEAD, HEAD)] = dot(probs_low, g).astype(BF)
    dk_ref[kh % 2, :, lanes(kh // 2 * HEAD, HEAD)] = dot(grad_scores, q).astype(BF)
    dq = dot(grad_scores, k, TN).astype(BF)
    dq_ref[:, lanes(kh * width, width)] = jnp.concatenate(
        [dq[i * SHORT_DEV : (i + 1) * SHORT_DEV] for i in range(GROUPS)], axis=1
    )


WIDE = 4 * CHUNK
STEPS = GROUPS // 4
OWN = NZH * CHUNK


def long_head(keys, hh, z_hi, q, g, k, v, dq, scores, grads, low, acc_k, acc_v, kt):
    chunks = keys // CHUNK
    head = lanes(hh * HEAD, HEAD)
    acc_k[0:keys, :] = jnp.zeros((keys, HEAD), F32)
    acc_v[0:keys, :] = jnp.zeros((keys, HEAD), F32)
    kt[:, 0:keys] = k[0:keys, head].T

    @pl.loop(0, STEPS)
    def _(p):
        col = lanes((hh * STEPS + p) * WIDE, WIDE)
        q4, g4 = q[:, col], g[:, col]
        qs = jnp.concatenate([q4[:, i * HEAD : (i + 1) * HEAD] for i in range(4)], axis=0)
        gs = jnp.concatenate([g4[:, i * HEAD : (i + 1) * HEAD] for i in range(4)], axis=0)
        top = None
        for n in range(chunks):
            at = slice(n * CHUNK, (n + 1) * CHUNK)
            s = dot(k[at, head], qs, NT)
            if n >= chunks - 2:
                key = lax.broadcasted_iota(jnp.int32, (CHUNK, WIDE), 0) + (n - chunks + 2) * CHUNK
                token = lax.broadcasted_iota(jnp.int32, (CHUNK, WIDE), 1) % CHUNK + z_hi * CHUNK
                s = jnp.where(key <= token, s, NEG)
            scores[at, :] = s
            m = jnp.max(s, axis=0, keepdims=True)
            top = m if top is None else jnp.maximum(top, m)
        total = None
        for n in range(chunks):
            at = slice(n * CHUNK, (n + 1) * CHUNK)
            e = jnp.exp2((scores[at, :] - top) * EXP_FACTOR)
            scores[at, :] = e
            part = jnp.sum(e, axis=0, keepdims=True)
            total = part if total is None else total + part
            grads[at, :] = dot(v[at, head], gs, NT)
        scale = 1.0 / total
        delta = None
        for n in range(chunks):
            at = slice(n * CHUNK, (n + 1) * CHUNK)
            pb = (scores[at, :] * scale).astype(BF)
            part = jnp.sum(pb.astype(F32) * grads[at, :], axis=0, keepdims=True)
            delta = part if delta is None else delta + part
            acc_v[at, :] += dot(pb, gs)
        scale = scale * FACTOR
        for n in range(chunks):
            at = slice(n * CHUNK, (n + 1) * CHUNK)
            ds = (scores[at, :] * scale * (grads[at, :] - delta)).astype(BF)
            low[at, :] = ds
            acc_k[at, :] += dot(ds, qs)
        out = dot(kt[:, 0:keys], low[0:keys, :]).astype(BF).T
        dq[:, col] = jnp.concatenate([out[i * CHUNK : (i + 1) * CHUNK] for i in range(4)], axis=1)


def fold(a):
    return jnp.concatenate([a[:, :128], a[:, 128:]], axis=0)


def kernel(
    q_hbm, g_hbm, k_hbm, v_hbm, x_hbm, seg_ref, master, first, second,
    gq, gv, new_master, new_first, new_second, new_weight,
    qs, gs, ks, vs, xs, xt, sdq, sgk, sgv,
    qb, gb, kb, vb, dq, scores, grads, low, acc_k, acc_v, kt, dks, dvs, totk, totv,
    rxk, rxv, zsk, zrk, zsv, zrv, gkl, gvl, xg, gk, wp, wr, wsum, zf, zp, zq, nwr,
    load_sem, own_sem, q_send, q_recv, kv_send, kv_recv, fw_send, fw_recv, dq_send, dq_recv,
    rk_send, rk_recv, rv_send, rv_recv, zk_send, zk_recv, zv_send, zv_recv, x_send, x_recv,
    s_send, s_recv, l_send, l_recv, v_send, v_recv, w_send, w_recv, p_send, p_recv,
    nz_send, nz_recv, ny_send, ny_recv,
):
    y, z_lo, x, z_hi, core = place()
    c = lax.axis_index("ctx")
    z = z_hi * NZL + z_lo
    other = 1 - core
    sibling = device(y, z_lo, x, z_hi, other)
    partner = device(y, z_lo, x, 1 - z_hi, core)
    early, late = pl.ds(0, LONG_DEV), pl.ds(LONG_DEV, SHORT_DEV)
    my_tokens = lanes(core * TOK_DEV, TOK_DEV)

    loads = [pltpu.make_async_copy(x_hbm, xs, load_sem.at[4])]
    loads += [
        pltpu.make_async_copy(hbm.at[late, :], vmem, load_sem.at[i])
        for i, (hbm, vmem) in enumerate(((q_hbm, qs), (g_hbm, gs), (k_hbm, ks), (v_hbm, vs)))
    ]
    own_rows = rows(c * LONG_DEV, LONG_DEV, 64)
    pair_rows = rows(core * LONG_DEV, LONG_DEV, 64)
    loads += [
        pltpu.make_async_copy(src.at[early, lanes(core * width, width)], dst.at[where, :], own_sem.at[i])
        for i, (src, dst, width, where) in enumerate(
            (
                (k_hbm, kb, HALF_K, own_rows),
                (v_hbm, vb, HALF_K, own_rows),
                (q_hbm, qb, HALF_Q, pair_rows),
                (g_hbm, gb, HALF_Q, pair_rows),
            )
        )
    ]
    for copy in loads:
        copy.start()

    def x_peer(dx, sign):
        return (x + sign * dx + NX) % NX

    def z_peer(dz, sign):
        return (z + sign * dz + NZ) % NZ

    def z_device(pz):
        return device(y, pz % NZL, x, pz // NZL, core)

    group = [(dy, dc) for dy in range(NY) for dc in range(NC) if (dy, dc) != (0, 0)]

    def group_peer(i, sign):
        dy, dc = group[i]
        return (y + sign * dy + NY) % NY, (core + dc) % NC

    peers = [device(y, z_lo, x_peer(dx, 1), z_hi, (core + dc) % NC) for dx in range(1, NX) for dc in range(NC)]
    peers += [z_device(z_peer(dz, 1)) for dz in range(1, NZ)]
    peers.append(device(y, z_lo, x, 1 - z_hi, other))
    for i in range(len(group)):
        py, pc = group_peer(i, 1)
        peers.append(device(py, z_lo, x, z_hi, pc))
    barrier = pltpu.get_barrier_semaphore()
    for peer in peers:
        pl.semaphore_signal(barrier, inc=1, device_id=peer, device_id_type=MESH)

    loads[0].wait()

    @pl.loop(0, D // 128)
    def _(i):
        at = i * 128
        xt[rows(at, 128, 128), :] = xs[:, lanes(at, 128)].T

    pl.semaphore_wait(barrier, len(peers))

    def kv_copies(px, pz, pc, slot, sending):
        if sending:
            col, where = pc, own_rows
        else:
            col, where = core, rows(((px * NZH + pz) * NC + pc) * LONG_DEV, LONG_DEV, 64)
        return [
            remote(
                src.at[early, lanes(col * HALF_K, HALF_K)], dst.at[where, :],
                kv_send.at[n, slot], kv_recv.at[n, slot], device(y, z_lo, px, pz, pc),
            )
            for n, (src, dst) in enumerate(((k_hbm, kb), (v_hbm, vb)))
        ]

    def partner_copies(dc, sending):
        return kv_copies(x, 1 - z_hi, (core + dc) % NC, dc, sending)

    def sibling_copies(sending):
        return kv_copies(x, z_hi, other, 2, sending)

    def x_copies(dx, dc, sending):
        return kv_copies(x + dx if sending else x - dx, z_hi, (core + dc) % NC, 1 + 2 * dx + dc, sending)

    for dc in range(NC):
        for copy in partner_copies(dc, True):
            copy.start()
    for dx in range(1, NX):

        @pl.when(x + dx < NX)
        def _():
            for dc in range(NC):
                for copy in x_copies(dx, dc, True):
                    copy.start()

    swaps = [
        remote(
            src.at[early, lanes(other * HALF_Q, HALF_Q)], dst.at[pair_rows, :], q_send.at[n], q_recv.at[n], sibling
        )
        for n, (src, dst) in enumerate(((q_hbm, qb), (g_hbm, gb)))
    ]
    for copy in sibling_copies(True) + swaps:
        copy.start()

    def x_copy(i, sign):
        py, pc = group_peer(i, sign)
        sy, sc = (y, core) if sign > 0 else (py, pc)
        return remote(
            xt.reshape(NX * NZH, NC, NY, 96, TOK_DEV).at[:, pc, py],
            xg.at[sy, :, :, lanes(sc * TOK_DEV, TOK_DEV)],
            x_send.at[i], x_recv.at[i], device(py, z_lo, x, z_hi, pc),
        )

    for i in range(len(group)):
        x_copy(i, 1).start()
    mine = [
        pltpu.make_async_copy(
            xt.reshape(NX * NZH, NC, NY, 96, TOK_DEV).at[:, core, y], xg.at[y, :, :, my_tokens], own_sem.at[4]
        )
    ]
    mine[0].start()

    for copy in loads[1:5]:
        copy.wait()
    bias = short_mask(seg_ref)

    def heads(start, stop):
        @pl.loop(start, stop)
        def _(kh):
            short_head(kh, bias, qs, gs, ks, vs, sdq, sgk, sgv)

    heads(0, SHORT_FIRST)
    for dc in range(NC):
        for copy in partner_copies(dc, False):
            copy.wait_recv()

    def forward(dx, sending):
        px = x + dx if sending else x - dx
        where = rows(((x if sending else px) * NZH + 1 - z_hi) * CHUNK, CHUNK, 128)
        return [
            remote(
                b.at[where, :], b.at[where, :], fw_send.at[n, dx - 1], fw_recv.at[n, dx - 1],
                device(y, z_lo, px, z_hi, core),
            )
            for n, b in enumerate((kb, vb))
        ]

    for dx in range(1, NX):

        @pl.when(x + dx < NX)
        def _():
            for copy in forward(dx, True):
                copy.start()

    heads(SHORT_FIRST, HK)

    def short_copy(i, sign):
        py, pc = group_peer(i, sign)
        sy, sc = (y, core) if sign > 0 else (py, pc)
        return remote(
            sgk, gk.at[:, sy, sc, late, :], s_send.at[i], s_recv.at[i], device(py, z_lo, x, z_hi, pc)
        )

    for i in range(len(group)):
        short_copy(i, 1).start()
    mine += [
        pltpu.make_async_copy(sgk, gk.at[:, y, core, late, :], own_sem.at[5]),
        pltpu.make_async_copy(sdq, gq.at[late, :], own_sem.at[6]),
        pltpu.make_async_copy(sgv, gv.at[late, :], own_sem.at[7]),
    ]
    for copy in mine[1:]:
        copy.start()

    for copy in loads[5:]:
        copy.wait()
    for copy in sibling_copies(False):
        copy.wait_recv()
    for dx in range(1, NX):

        @pl.when(x >= dx)
        def _():
            for dc in range(NC):
                for copy in x_copies(dx, dc, False):
                    copy.wait_recv()
            for copy in forward(dx, False):
                copy.wait_recv()

    for copy in swaps:
        copy.wait()

    def rk_copy(hh, dx, sending):
        px = x - dx if sending else x + dx
        at = rows((px if sending else x) * OWN, OWN, 256)
        return remote(
            dks.at[hh, at, :], rxk.at[dx - 1, hh], rk_send.at[hh, dx - 1], rk_recv.at[hh, dx - 1],
            device(y, z_lo, px, z_hi, core),
        )

    def rv_copy(dx, sending):
        px = x - dx if sending else x + dx
        at = rows((px if sending else x) * OWN, OWN, 256)
        return remote(
            dvs.at[:, at, :], rxv.at[dx - 1], rv_send.at[dx - 1], rv_recv.at[dx - 1],
            device(y, z_lo, px, z_hi, core),
        )

    def zk_copy(hh):
        return remote(zsk.at[hh], zrk.at[hh], zk_send.at[hh], zk_recv.at[hh], partner)

    zv_copy = remote(zsv, zrv, zv_send.at[0], zv_recv.at[0], partner)
    ours = rows(z_hi * CHUNK, CHUNK, 128)
    theirs = rows((1 - z_hi) * CHUNK, CHUNK, 128)

    @pl.loop(0, 2)
    def _(hh):
        for n in range(NX):

            @pl.when(x == n)
            def _():
                keys, below = (n + 1) * OWN, n * OWN
                long_head(keys, hh, z_hi, qb, gb, kb, vb, dq, scores, grads, low, acc_k, acc_v, kt)
                if below:
                    dks[hh, 0:below, :] = acc_k[0:below, :].astype(BF)
                totk[hh] = acc_k[below:keys, :]
                if below:
                    dvs[hh, 0:below, :] = acc_v[0:below, :].astype(BF)
                totv[hh] = acc_v[below:keys, :]

        for dx in range(1, NX):

            @pl.when(x >= dx)
            def _():
                rk_copy(hh, dx, True).start()

        @pl.when(x == NX - 1)
        def _():
            zsk[hh] = totk[hh, theirs, :].astype(BF)
            zk_copy(hh).start()

    for dx in range(1, NX):

        @pl.when(x >= dx)
        def _():
            rv_copy(dx, True).start()

    dq_copy = remote(
        dq.at[rows(other * LONG_DEV, LONG_DEV, 64), :], gq.at[early, lanes(core * HALF_Q, HALF_Q)],
        dq_send.at[0], dq_recv.at[0], sibling,
    )
    dq_copy.start()
    mine.append(
        pltpu.make_async_copy(dq.at[pair_rows, :], gq.at[early, lanes(core * HALF_Q, HALF_Q)], own_sem.at[8])
    )
    mine[-1].start()

    def sum_over_x(hh):
        @pl.when(x < NX - 1)
        def _():
            for dx in range(1, NX):

                @pl.when(x + dx < NX)
                def _():
                    rk_copy(hh, dx, False).wait_recv()
                    totk[hh] += rxk[dx - 1, hh].astype(F32)

            zsk[hh] = totk[hh, theirs, :].astype(BF)
            zk_copy(hh).start()

    def long_copy(hh, i, sign):
        py, pc = group_peer(i, sign)
        sy, sc = (y, core) if sign > 0 else (py, pc)
        return remote(
            gkl.at[hh], gk.at[hh, sy, :, early, lanes(sc * HEAD, HEAD)], l_send.at[hh, i], l_recv.at[hh, i],
            device(py, z_lo, x, z_hi, pc),
        )

    def spread(hh):
        zk_copy(hh).wait_recv()
        both = (totk[hh, ours, :] + zrk[hh].astype(F32)).astype(BF)
        gkl[hh, 0] = both[:LONG_DEV]
        gkl[hh, 1] = both[LONG_DEV:]
        for i in range(len(group)):
            long_copy(hh, i, 1).start()
        copy = pltpu.make_async_copy(
            gkl.at[hh], gk.at[hh, y, :, early, lanes(core * HEAD, HEAD)], own_sem.at[9 + hh]
        )
        copy.start()
        return copy

    def w_copy(hh, dx, sign):
        px = x_peer(dx, sign)
        return remote(
            wp.at[hh, px], wr.at[hh, dx - 1], w_send.at[hh, dx - 1], w_recv.at[hh, dx - 1],
            device(y, z_lo, px, z_hi, core),
        )

    def product(hh, px):
        result = None
        for sy in range(NY):
            left = xg[sy, rows(NZH * px, NZH, 1)].reshape(NZH * 96, NC * TOK_DEV)
            term = dot(left, gk[hh, sy].reshape(NC * TOK_DEV, HALF_K))
            result = term if result is None else result + term
        return result.reshape(NZH, 96, HALF_K)

    def multiply(hh, own):
        own.wait()
        for i in range(len(group)):
            long_copy(hh, i, -1).wait_recv()
        for dx in (2, 1, 3):
            px = x_peer(dx, 1)
            wp[hh, px] = product(hh, px).astype(BF)
            w_copy(hh, dx, 1).start()
        wsum[hh] = product(hh, x)

    def p_copy(hh, dz, sign):
        pz = z_peer(dz, sign)
        return remote(
            zp.at[hh, pz], zq.at[hh, dz - 1], p_send.at[hh, dz - 1], p_recv.at[hh, dz - 1], z_device(pz)
        )

    def reduce_x(hh):
        for dx in (1, 3, 2):
            w_copy(hh, dx, -1).wait_recv()
            wsum[hh] += wr[hh, dx - 1].astype(F32)
        for pz in range(NZ):
            zf[hh, pz] = fold(wsum[hh, pz // NZL, (pz % NZL) * 24 : (pz % NZL + 1) * 24, :])
        zp[hh] = zf[hh].astype(BF)
        for dz in (4, 3, 5, 2, 6, 1, 7):
            p_copy(hh, dz, 1).start()

    d = lax.axis_index("dp")

    def nz_copy(hh, dz, sign):
        pz = (z_lo + sign * dz + NZL) % NZL
        slot = d if sign > 0 else y * NZL + pz
        return remote(
            nwr.at[hh, slot], nwr.at[hh, slot], nz_send.at[hh, dz - 1], nz_recv.at[hh, dz - 1],
            device(y, pz, x, z_hi, core),
        )

    def ny_copy(hh, dy, dz, sign):
        py = (y + sign * dy + NY) % NY
        slot = (y if sign > 0 else py) * NZL + (z_lo - dz + NZL) % NZL
        return remote(
            nwr.at[hh, slot], nwr.at[hh, slot], ny_send.at[hh, dy - 1, dz], ny_recv.at[hh, dy - 1, dz],
            device(py, z_lo, x, z_hi, core),
        )

    def update(hh):
        share = zf[hh, z]
        for dz in range(1, NZ):
            p_copy(hh, dz, -1).wait_recv()
            share = share + zq[hh, dz - 1].astype(F32)
        share = share * (1.0 / (TOK_DEV * NY * NZ * NX * NC))
        fresh = []
        for b in range(2):
            col = slice((2 * b + hh) * 128, (2 * b + hh + 1) * 128)
            grad = share[b * 24 : (b + 1) * 24]
            moment = BETA_ONE * first[0, :, col] + (1.0 - BETA_ONE) * grad
            square = BETA_TWO * second[0, :, col] + (1.0 - BETA_TWO) * grad * grad
            first_hat = moment / (1.0 - BETA_ONE**STEP_COUNT)
            second_hat = square / (1.0 - BETA_TWO**STEP_COUNT)
            old = master[0, :, col]
            new = old - LEARN_RATE * (first_hat / (jnp.sqrt(second_hat) + ADAM_EPS) + DECAY * old)
            new_first[0, :, col] = moment
            new_second[0, :, col] = square
            new_master[0, :, col] = new
            fresh.append(new)
        nwr[hh, d] = jnp.concatenate(fresh, axis=0).astype(BF)
        for dz in range(1, NZL):
            nz_copy(hh, dz, 1).start()
        for dy in range(1, NY):
            ny_copy(hh, dy, 0, 1).start()

    def pass_on(hh):
        for dz in (1, 3, 2):
            nz_copy(hh, dz, -1).wait_recv()
            for dy in (2, 1, 3):
                ny_copy(hh, dy, dz, 1).start()

    def finish(hh):
        for dy in range(1, NY):
            for dz in range(NZL):
                ny_copy(hh, dy, dz, -1).wait_recv()
        for pair in range(NY * NZL // 2):
            two = [nwr[hh, 2 * pair + i].astype(F32) for i in range(2)]
            for b in range(2):
                both = jnp.concatenate([t[b * 24 : (b + 1) * 24] for t in two], axis=0)
                new_weight[0, pair * 48 : (pair + 1) * 48, (2 * b + hh) * 128 : (2 * b + hh + 1) * 128] = both.astype(BF)

    sum_over_x(0)
    own = spread(0)
    sum_over_x(1)
    mine[0].wait()
    mine[1].wait()
    for i in range(len(group)):
        x_copy(i, -1).wait_recv()
        short_copy(i, -1).wait_recv()
    multiply(0, own)
    own = spread(1)

    @pl.when(x < NX - 1)
    def _():
        for dx in range(1, NX):

            @pl.when(x + dx < NX)
            def _():
                rv_copy(dx, False).wait_recv()
                totv[...] += rxv[dx - 1].astype(F32)

    zsv[...] = totv[:, theirs, :].astype(BF)
    zv_copy.start()
    multiply(1, own)
    reduce_x(0)
    zv_copy.wait_recv()
    for hh in range(2):
        both = (totv[hh, ours, :] + zrv[hh].astype(F32)).astype(BF)
        gvl[0, :, hh * HEAD : (hh + 1) * HEAD] = both[:LONG_DEV]
        gvl[1, :, hh * HEAD : (hh + 1) * HEAD] = both[LONG_DEV:]
    my_keys = lanes(core * HALF_K, HALF_K)
    v_copy = remote(gvl.at[other], gv.at[early, my_keys], v_send.at[0], v_recv.at[0], sibling)
    v_copy.start()
    mine.append(pltpu.make_async_copy(gvl.at[core], gv.at[early, my_keys], own_sem.at[11]))
    mine[-1].start()
    update(0)
    reduce_x(1)
    pass_on(0)
    update(1)
    pass_on(1)
    finish(0)
    finish(1)

    for copy in mine[2:]:
        copy.wait()
    v_copy.wait()
    dq_copy.wait()
    zv_copy.wait_send()
    for copy in sibling_copies(True):
        copy.wait_send()
    for dc in range(NC):
        for copy in partner_copies(dc, True):
            copy.wait_send()
    for dx in range(1, NX):

        @pl.when(x + dx < NX)
        def _():
            for dc in range(NC):
                for copy in x_copies(dx, dc, True):
                    copy.wait_send()
            for copy in forward(dx, True):
                copy.wait_send()

        @pl.when(x >= dx)
        def _():
            for hh in range(2):
                rk_copy(hh, dx, True).wait_send()
            rv_copy(dx, True).wait_send()

    for i in range(len(group)):
        x_copy(i, 1).wait_send()
        short_copy(i, 1).wait_send()
    for hh in range(2):
        zk_copy(hh).wait_send()
        for i in range(len(group)):
            long_copy(hh, i, 1).wait_send()
        for dx in range(1, NX):
            w_copy(hh, dx, 1).wait_send()
        for dz in range(1, NZ):
            p_copy(hh, dz, 1).wait_send()
        for dz in range(1, NZL):
            nz_copy(hh, dz, 1).wait_send()
        for dy in range(1, NY):
            for dz in range(NZL):
                ny_copy(hh, dy, dz, 1).wait_send()


HBM = pl.BlockSpec(memory_space=pltpu.HBM)
VMEM = pl.BlockSpec(memory_space=pltpu.VMEM)
DMA = pltpu.SemaphoreType.DMA


def array(shape, dtype=BF):
    return jax.ShapeDtypeStruct(shape, dtype)


STORE_CUTS = 4


def store_kernel(*refs):
    sources, targets, held, (sem_in, sem_out) = refs[:6], refs[6:12], refs[12:18], refs[18:]
    cut = TOK_DEV // STORE_CUTS
    parts = [(0, pl.ds(i * cut, cut)) for i in range(STORE_CUTS)] + [(i, pl.ds(0, n)) for i, n in ((1, TOK_DEV), (2, 1), (3, 1), (4, 1), (5, 1))]
    loads = [
        pltpu.make_async_copy(sources[i].at[at], held[i].at[at], sem_in.at[n]) for n, (i, at) in enumerate(parts)
    ]
    stores = [
        pltpu.make_async_copy(held[i].at[at], targets[i].at[at], sem_out.at[n]) for n, (i, at) in enumerate(parts)
    ]
    for copy in loads:
        copy.start()
    for load, store in zip(loads, stores):
        load.wait()
        store.start()
    for copy in stores:
        copy.wait()


def on_device(
    layer_inputs, queries, key_states, value_states, output_grad, short_segments, master, first_moment, second_moment
):
    keys = NX * OWN
    tile = (1, 24, KD)
    pairs = lambda *shape: [DMA(shape), DMA(shape)]
    results = [
        array((TOK_DEV, QD)),
        array((TOK_DEV, KD)),
        array(tile, F32),
        array(tile, F32),
        array(tile, F32),
        array((1, 384, KD)),
    ]
    made = pl.pallas_call(
        kernel,
        name="step",
        out_shape=results,
        in_specs=[HBM] * 5 + [VMEM] * 4,
        out_specs=[HBM] * 2 + [VMEM] * 4,
        scratch_shapes=[
            pltpu.VMEM((SHORT_DEV, QD), BF),
            pltpu.VMEM((SHORT_DEV, QD), BF),
            pltpu.VMEM((SHORT_DEV, KD), BF),
            pltpu.VMEM((SHORT_DEV, KD), BF),
            pltpu.VMEM((TOK_DEV, D), BF),
            pltpu.VMEM((D, TOK_DEV), BF),
            pltpu.VMEM((SHORT_DEV, QD), BF),
            pltpu.VMEM((2, SHORT_DEV, HALF_K), BF),
            pltpu.VMEM((SHORT_DEV, KD), BF),
            pltpu.VMEM((CHUNK, HALF_Q), BF),
            pltpu.VMEM((CHUNK, HALF_Q), BF),
            pltpu.VMEM((keys, HALF_K), BF),
            pltpu.VMEM((keys, HALF_K), BF),
            pltpu.VMEM((CHUNK, HALF_Q), BF),
            pltpu.VMEM((keys, WIDE), F32),
            pltpu.VMEM((keys, WIDE), F32),
            pltpu.VMEM((keys, WIDE), BF),
            pltpu.VMEM((keys, HEAD), F32),
            pltpu.VMEM((keys, HEAD), F32),
            pltpu.VMEM((HEAD, keys), BF),
            pltpu.VMEM((2, keys, HEAD), BF),
            pltpu.VMEM((2, keys, HEAD), BF),
            pltpu.VMEM((2, OWN, HEAD), F32),
            pltpu.VMEM((2, OWN, HEAD), F32),
            pltpu.VMEM((NX - 1, 2, OWN, HEAD), BF),
            pltpu.VMEM((NX - 1, 2, OWN, HEAD), BF),
            pltpu.VMEM((2, CHUNK, HEAD), BF),
            pltpu.VMEM((2, CHUNK, HEAD), BF),
            pltpu.VMEM((2, CHUNK, HEAD), BF),
            pltpu.VMEM((2, CHUNK, HEAD), BF),
            pltpu.VMEM((2, NC, LONG_DEV, HEAD), BF),
            pltpu.VMEM((NC, LONG_DEV, HALF_K), BF),
            pltpu.VMEM((NY, NX * NZH, 96, NC * TOK_DEV), BF),
            pltpu.VMEM((2, NY, NC, TOK_DEV, HALF_K), BF),
            pltpu.VMEM((2, NX, NZH, 96, HALF_K), BF),
            pltpu.VMEM((2, NX - 1, NZH, 96, HALF_K), BF),
            pltpu.VMEM((2, NZH, 96, HALF_K), F32),
            pltpu.VMEM((2, NZ, 48, 128), F32),
            pltpu.VMEM((2, NZ, 48, 128), BF),
            pltpu.VMEM((2, NZ - 1, 48, 128), BF),
            pltpu.VMEM((2, NY * NZL, 48, 128), BF),
            DMA((5,)),
            DMA((12,)),
            *pairs(2),
            *pairs(2, 9),
            *pairs(2, 3),
            *pairs(1),
            *pairs(2, 3),
            *pairs(3),
            *pairs(2),
            *pairs(1),
            *pairs(7),
            *pairs(7),
            *pairs(2, 7),
            *pairs(1),
            *pairs(2, 3),
            *pairs(2, 7),
            *pairs(2, 3),
            *pairs(2, 3, 4),
        ],
        compiler_params=pltpu.CompilerParams(
            vmem_limit_bytes=VMEM_LIMIT, collective_id=1, has_side_effects=True
        ),
    )(
        queries, output_grad, key_states, value_states, layer_inputs, short_segments,
        master, first_moment, second_moment,
    )
    return pl.pallas_call(
        store_kernel,
        name="store",
        out_shape=results,
        in_specs=[HBM] * 6,
        out_specs=[HBM] * 6,
        scratch_shapes=[pltpu.VMEM(r.shape, r.dtype) for r in results]
        + [DMA((STORE_CUTS + 5,)), DMA((STORE_CUTS + 5,))],
        compiler_params=pltpu.CompilerParams(vmem_limit_bytes=VMEM_LIMIT),
    )(*made)


def solution(mesh):
    tokens = P(("dp", "ctx"), None)
    shard = P("ctx", "dp", None)
    return jax.shard_map(
        on_device,
        mesh=mesh,
        in_specs=(tokens,) * 6 + (shard,) * 3,
        out_specs=(tokens, tokens, shard, shard, shard, P("ctx", None, None)),
        check_vma=False,
    )
```

profile of v0, /device:TPU:2, one launch (start us, length us, event | category | flops | bytes accessed | tf_op | source)
XLA Modules:
  0.0 81.1 jit_solution(2713152163977682941)
XLA Ops:
  0.6 78.0 %step.1 = (bf16[128,6144]{1,0:T(8,128)(2,1)}, bf16[128,512]{1,0:T(8,128)(2,1)}, f32[1,24,512]{2,1,0:T(8,128)}, f32[1,24,512]{2,1,0:T(8,128)}, f32[1,24,512]{2,1,0:T(8,128)}, /*index=5*/bf16[1,384,512]{2,1,0:T(8,128)(2,1)}) custom-call(bf16[128,6144]{1,0:T(8,128)(2,1)} %q_hbm.1, bf16[128,6144]{1,0:T(8,128)(2,1)} %g_hbm.1, bf16[128,512]{1,0:T(8,128)(2,1)} %k_hbm.1, ...), custom_call_target="tpu_custom_call" | custom-call | tf_op jit(solution)/shard_map/step/pallas_call | solution.py:703
  78.6 2.5 %store.1 = (bf16[128,6144]{1,0:T(8,128)(2,1)}, bf16[128,512]{1,0:T(8,128)(2,1)}, f32[1,24,512]{2,1,0:T(8,128)}, f32[1,24,512]{2,1,0:T(8,128)}, f32[1,24,512]{2,1,0:T(8,128)}, /*index=5*/bf16[1,384,512]{2,1,0:T(8,128)(2,1)}) custom-call(bf16[128,6144]{1,0:T(8,128)(2,1)} %get-tuple-element.12.refs_0_, bf16[128,512]{1,0:T(8,128)(2,1)} %get-tuple-element.13.refs_1_, ...), custom_call_target="tpu_custom_call" | custom-call | tf_op jit(solution)/shard_map/store/pallas_call | solution.py:777
where the time goes:
time: 81.7 us; the launch traced here: 81.1 us
  Pallas kernels  80.5 us (99%)
    pallas_call x1, Pallas kernels, on_device(): pl.pallas_call(kernel, name='step', out_shape=results, in_specs=[HBM] * 5...  78 us
    pallas_call x1, Pallas kernels, on_device(): pl.pallas_call(store_kernel, name='store', out_shape=results, in_specs=[H...  2.51 us

commit v1 on v0

--- a/solution.py
+++ b/solution.py
@@ -11,7 +11,7 @@
 HEAD = 128
 GROUPS = 12
 HK = 4
-SHORT_FIRST = 2
+SHORT_FIRST = 3
 LONG_DEV = 64
 SHORT_DEV = 64
 TOK_DEV = 128
@@ -112,23 +112,21 @@
 OWN = NZH * CHUNK
 
 
-def long_head(keys, hh, z_hi, q, g, k, v, dq, scores, grads, low, acc_k, acc_v, kt):
+def long_head(keys, hh, z_hi, q, g, kv, scores, grads, probs, low, acc_k):
     chunks = keys // CHUNK
-    head = lanes(hh * HEAD, HEAD)
     acc_k[0:keys, :] = jnp.zeros((keys, HEAD), F32)
-    acc_v[0:keys, :] = jnp.zeros((keys, HEAD), F32)
-    kt[:, 0:keys] = k[0:keys, head].T
 
     @pl.loop(0, STEPS)
     def _(p):
         col = lanes((hh * STEPS + p) * WIDE, WIDE)
+        wide = lanes(p * WIDE, WIDE)
         q4, g4 = q[:, col], g[:, col]
         qs = jnp.concatenate([q4[:, i * HEAD : (i + 1) * HEAD] for i in range(4)], axis=0)
         gs = jnp.concatenate([g4[:, i * HEAD : (i + 1) * HEAD] for i in range(4)], axis=0)
         top = None
         for n in range(chunks):
             at = slice(n * CHUNK, (n + 1) * CHUNK)
-            s = dot(k[at, head], qs, NT)
+            s = dot(kv[hh, at, :HEAD], qs, NT)
             if n >= chunks - 2:
                 key = lax.broadcasted_iota(jnp.int32, (CHUNK, WIDE), 0) + (n - chunks + 2) * CHUNK
                 token = lax.broadcasted_iota(jnp.int32, (CHUNK, WIDE), 1) % CHUNK + z_hi * CHUNK
@@ -136,30 +134,42 @@
             scores[at, :] = s
             m = jnp.max(s, axis=0, keepdims=True)
             top = m if top is None else jnp.maximum(top, m)
-        total = None
+        total = delta = None
         for n in range(chunks):
             at = slice(n * CHUNK, (n + 1) * CHUNK)
             e = jnp.exp2((scores[at, :] - top) * EXP_FACTOR)
             scores[at, :] = e
+            dp = dot(kv[hh, at, HEAD:], gs, NT)
+            grads[at, :] = dp
             part = jnp.sum(e, axis=0, keepdims=True)
             total = part if total is None else total + part
-            grads[at, :] = dot(v[at, head], gs, NT)
+            part = jnp.sum(e * dp, axis=0, keepdims=True)
+            delta = part if delta is None else delta + part
         scale = 1.0 / total
-        delta = None
+        delta = delta * scale
         for n in range(chunks):
             at = slice(n * CHUNK, (n + 1) * CHUNK)
-            pb = (scores[at, :] * scale).astype(BF)
-            part = jnp.sum(pb.astype(F32) * grads[at, :], axis=0, keepdims=True)
-            delta = part if delta is None else delta + part
-            acc_v[at, :] += dot(pb, gs)
-        scale = scale * FACTOR
-        for n in range(chunks):
-            at = slice(n * CHUNK, (n + 1) * CHUNK)
-            ds = (scores[at, :] * scale * (grads[at, :] - delta)).astype(BF)
-            low[at, :] = ds
+            pr = scores[at, :] * scale
+            probs[hh, at, wide] = pr.astype(BF)
+            ds = (pr * ((grads[at, :] - delta) * FACTOR)).astype(BF)
+            low[hh, at, wide] = ds
             acc_k[at, :] += dot(ds, qs)
-        out = dot(kt[:, 0:keys], low[0:keys, :]).astype(BF).T
-        dq[:, col] = jnp.concatenate([out[i * CHUNK : (i + 1) * CHUNK] for i in range(4)], axis=1)
+
+
+def long_rest(keys, hh, g, kv, dq, probs, low, acc_v):
+    width = GROUPS * HEAD
+    col = lanes(hh * width, width)
+    gr = g[:, col]
+    gs = jnp.concatenate([gr[:, i * HEAD : (i + 1) * HEAD] for i in range(GROUPS)], axis=0)
+    for n in range(keys // CHUNK):
+        at = slice(n * CHUNK, (n + 1) * CHUNK)
+        acc_v[at, :] = dot(probs[hh, at, :], gs)
+    kt = kv[hh, 0:keys, :HEAD].T
+    for p in range(STEPS):
+        out = dot(kt, low[hh, 0:keys, p * WIDE : (p + 1) * WIDE]).astype(BF).T
+        dq[:, lanes(hh * width + p * WIDE, WIDE)] = jnp.concatenate(
+            [out[i * CHUNK : (i + 1) * CHUNK] for i in range(4)], axis=1
+        )
 
 
 def fold(a):
@@ -167,12 +177,13 @@
 
 
 def kernel(
-    q_hbm, g_hbm, k_hbm, v_hbm, x_hbm, seg_ref, master, first, second,
-    gq, gv, new_master, new_first, new_second, new_weight,
+    q_hbm, g_hbm, k_hbm, v_hbm, x_hbm, seg_hbm, master_hbm, first_hbm, second_hbm,
+    gq, gv, master_out, first_out, second_out, weight_out,
+    seg_ref, master, first, second, new_master, new_first, new_second, new_weight, kvs,
     qs, gs, ks, vs, xs, xt, sdq, sgk, sgv,
-    qb, gb, kb, vb, dq, scores, grads, low, acc_k, acc_v, kt, dks, dvs, totk, totv,
+    qb, gb, kvb, dq, scores, grads, probs, low, acc_k, acc_v, dks, dvs, totk, totv,
     rxk, rxv, zsk, zrk, zsv, zrv, gkl, gvl, xg, gk, wp, wr, wsum, zf, zp, zq, nwr,
-    load_sem, own_sem, q_send, q_recv, kv_send, kv_recv, fw_send, fw_recv, dq_send, dq_recv,
+    load_sem, key_sem, own_sem, out_sem, q_send, q_recv, kv_send, kv_recv, fw_send, fw_recv, dq_send, dq_recv,
     rk_send, rk_recv, rv_send, rv_recv, zk_send, zk_recv, zv_send, zv_recv, x_send, x_recv,
     s_send, s_recv, l_send, l_recv, v_send, v_recv, w_send, w_recv, p_send, p_recv,
     nz_send, nz_recv, ny_send, ny_recv,
@@ -186,25 +197,37 @@
     early, late = pl.ds(0, LONG_DEV), pl.ds(LONG_DEV, SHORT_DEV)
     my_tokens = lanes(core * TOK_DEV, TOK_DEV)
 
-    loads = [pltpu.make_async_copy(x_hbm, xs, load_sem.at[4])]
-    loads += [
-        pltpu.make_async_copy(hbm.at[late, :], vmem, load_sem.at[i])
-        for i, (hbm, vmem) in enumerate(((q_hbm, qs), (g_hbm, gs), (k_hbm, ks), (v_hbm, vs)))
-    ]
     own_rows = rows(c * LONG_DEV, LONG_DEV, 64)
     pair_rows = rows(core * LONG_DEV, LONG_DEV, 64)
-    loads += [
-        pltpu.make_async_copy(src.at[early, lanes(core * width, width)], dst.at[where, :], own_sem.at[i])
-        for i, (src, dst, width, where) in enumerate(
+    keyed = [
+        pltpu.make_async_copy(
+            src.at[early, pl.ds((2 * to + hh) * HEAD, HEAD)],
+            kvs.at[to, hh, :, pl.ds(n * HEAD, HEAD)],
+            key_sem.at[4 * to + 2 * hh + n],
+        )
+        for hh in range(2)
+        for to in range(NC)
+        for n, src in enumerate((k_hbm, v_hbm))
+    ]
+    loads = [
+        pltpu.make_async_copy(hbm, vmem, load_sem.at[i])
+        for i, (hbm, vmem) in enumerate(
             (
-                (k_hbm, kb, HALF_K, own_rows),
-                (v_hbm, vb, HALF_K, own_rows),
-                (q_hbm, qb, HALF_Q, pair_rows),
-                (g_hbm, gb, HALF_Q, pair_rows),
+                (x_hbm, xs),
+                (q_hbm.at[late, :], qs),
+                (g_hbm.at[late, :], gs),
+                (k_hbm.at[late, :], ks),
+                (v_hbm.at[late, :], vs),
+                (seg_hbm, seg_ref),
+                (q_hbm.at[early, lanes(core * HALF_Q, HALF_Q)], qb.at[pair_rows, :]),
+                (g_hbm.at[early, lanes(core * HALF_Q, HALF_Q)], gb.at[pair_rows, :]),
+                (master_hbm, master),
+                (first_hbm, first),
+                (second_hbm, second),
             )
         )
     ]
-    for copy in loads:
+    for copy in keyed + loads:
         copy.start()
 
     def x_peer(dx, sign):
@@ -222,9 +245,9 @@
         dy, dc = group[i]
         return (y + sign * dy + NY) % NY, (core + dc) % NC
 
-    peers = [device(y, z_lo, x_peer(dx, 1), z_hi, (core + dc) % NC) for dx in range(1, NX) for dc in range(NC)]
-    peers += [z_device(z_peer(dz, 1)) for dz in range(1, NZ)]
-    peers.append(device(y, z_lo, x, 1 - z_hi, other))
+    peers = [device(y, z_lo, x, 1 - z_hi, other)]
+    peers += [z_device(z_peer(dz, 1)) for dz in (4, 3, 5, 2, 6, 1, 7)]
+    peers += [device(y, z_lo, x_peer(dx, 1), z_hi, (core + dc) % NC) for dx in (2, 1, 3) for dc in (1, 0)]
     for i in range(len(group)):
         py, pc = group_peer(i, 1)
         peers.append(device(py, z_lo, x, z_hi, pc))
@@ -234,45 +257,56 @@
 
     loads[0].wait()
 
-    @pl.loop(0, D // 128)
+    @pl.loop(0, D // 1024)
     def _(i):
-        at = i * 128
-        xt[rows(at, 128, 128), :] = xs[:, lanes(at, 128)].T
-
+        for j in range(8):
+            at = i * 1024 + j * 128
+            xt[rows(at, 128, 128), :] = xs[:, lanes(at, 128)].T
+
+    for copy in loads[1:6]:
+        copy.wait()
+    bias = short_mask(seg_ref)
+
+    def heads(start, stop):
+        @pl.loop(start, stop)
+        def _(kh):
+            short_head(kh, bias, qs, gs, ks, vs, sdq, sgk, sgv)
+
+    heads(0, SHORT_FIRST)
+    for copy in keyed:
+        copy.wait()
+    own_kv = pltpu.make_async_copy(kvs.at[core], kvb.at[:, own_rows, :], own_sem.at[4])
+    own_kv.start()
     pl.semaphore_wait(barrier, len(peers))
 
-    def kv_copies(px, pz, pc, slot, sending):
-        if sending:
-            col, where = pc, own_rows
-        else:
-            col, where = core, rows(((px * NZH + pz) * NC + pc) * LONG_DEV, LONG_DEV, 64)
-        return [
-            remote(
-                src.at[early, lanes(col * HALF_K, HALF_K)], dst.at[where, :],
-                kv_send.at[n, slot], kv_recv.at[n, slot], device(y, z_lo, px, pz, pc),
-            )
-            for n, (src, dst) in enumerate(((k_hbm, kb), (v_hbm, vb)))
-        ]
-
-    def partner_copies(dc, sending):
-        return kv_copies(x, 1 - z_hi, (core + dc) % NC, dc, sending)
-
-    def sibling_copies(sending):
-        return kv_copies(x, z_hi, other, 2, sending)
-
-    def x_copies(dx, dc, sending):
-        return kv_copies(x + dx if sending else x - dx, z_hi, (core + dc) % NC, 1 + 2 * dx + dc, sending)
-
-    for dc in range(NC):
-        for copy in partner_copies(dc, True):
-            copy.start()
-    for dx in range(1, NX):
-
-        @pl.when(x + dx < NX)
-        def _():
-            for dc in range(NC):
-                for copy in x_copies(dx, dc, True):
-                    copy.start()
+    def kv_copy(hh, px, pz, pc, slot, sending):
+        where = own_rows if sending else rows(((px * NZH + pz) * NC + pc) * LONG_DEV, LONG_DEV, 64)
+        return remote(
+            kvs.at[pc if sending else core, hh], kvb.at[hh, where, :], kv_send.at[hh, slot], kv_recv.at[hh, slot],
+            device(y, z_lo, px, pz, pc),
+        )
+
+    def partner_copy(hh, dc, sending):
+        return kv_copy(hh, x, 1 - z_hi, (core + dc) % NC, dc, sending)
+
+    def sibling_copy(hh, sending):
+        return kv_copy(hh, x, z_hi, other, 2, sending)
+
+    def near_copy(hh, dx, dc, sending):
+        return kv_copy(hh, x + dx if sending else x - dx, z_hi, (core + dc) % NC, 1 + 2 * dx + dc, sending)
+
+    for hh in range(2):
+        for dc in range(NC):
+            partner_copy(hh, dc, True).start()
+    for hh in range(2):
+        for dx in range(1, NX):
+
+            @pl.when(x + dx < NX)
+            def _():
+                for dc in range(NC):
+                    near_copy(hh, dx, dc, True).start()
+
+        sibling_copy(hh, True).start()
 
     swaps = [
         remote(
@@ -280,7 +314,7 @@
         )
         for n, (src, dst) in enumerate(((q_hbm, qb), (g_hbm, gb)))
     ]
-    for copy in sibling_copies(True) + swaps:
+    for copy in swaps:
         copy.start()
 
     def x_copy(i, sign):
@@ -296,42 +330,28 @@
         x_copy(i, 1).start()
     mine = [
         pltpu.make_async_copy(
-            xt.reshape(NX * NZH, NC, NY, 96, TOK_DEV).at[:, core, y], xg.at[y, :, :, my_tokens], own_sem.at[4]
+            xt.reshape(NX * NZH, NC, NY, 96, TOK_DEV).at[:, core, y], xg.at[y, :, :, my_tokens], own_sem.at[5]
         )
     ]
     mine[0].start()
 
-    for copy in loads[1:5]:
-        copy.wait()
-    bias = short_mask(seg_ref)
-
-    def heads(start, stop):
-        @pl.loop(start, stop)
-        def _(kh):
-            short_head(kh, bias, qs, gs, ks, vs, sdq, sgk, sgv)
-
-    heads(0, SHORT_FIRST)
-    for dc in range(NC):
-        for copy in partner_copies(dc, False):
-            copy.wait_recv()
-
-    def forward(dx, sending):
+    def forward(hh, dx, dc, sending):
         px = x + dx if sending else x - dx
-        where = rows(((x if sending else px) * NZH + 1 - z_hi) * CHUNK, CHUNK, 128)
-        return [
-            remote(
-                b.at[where, :], b.at[where, :], fw_send.at[n, dx - 1], fw_recv.at[n, dx - 1],
-                device(y, z_lo, px, z_hi, core),
-            )
-            for n, b in enumerate((kb, vb))
-        ]
-
-    for dx in range(1, NX):
-
-        @pl.when(x + dx < NX)
-        def _():
-            for copy in forward(dx, True):
-                copy.start()
+        chip = (x if sending else px) * NZH + 1 - z_hi
+        where = rows((chip * NC + (core + dc) % NC) * LONG_DEV, LONG_DEV, 64)
+        return remote(
+            kvb.at[hh, where, :], kvb.at[hh, where, :], fw_send.at[hh, dc, dx - 1], fw_recv.at[hh, dc, dx - 1],
+            device(y, z_lo, px, z_hi, core),
+        )
+
+    for hh in range(2):
+        for dc in range(NC):
+            partner_copy(hh, dc, False).wait_recv()
+            for dx in range(1, NX):
+
+                @pl.when(x + dx < NX)
+                def _():
+                    forward(hh, dx, dc, True).start()
 
     heads(SHORT_FIRST, HK)
 
@@ -345,36 +365,25 @@
     for i in range(len(group)):
         short_copy(i, 1).start()
     mine += [
-        pltpu.make_async_copy(sgk, gk.at[:, y, core, late, :], own_sem.at[5]),
-        pltpu.make_async_copy(sdq, gq.at[late, :], own_sem.at[6]),
-        pltpu.make_async_copy(sgv, gv.at[late, :], own_sem.at[7]),
+        pltpu.make_async_copy(sgk, gk.at[:, y, core, late, :], own_sem.at[6]),
+        pltpu.make_async_copy(sdq, gq.at[late, :], own_sem.at[7]),
+        pltpu.make_async_copy(sgv, gv.at[late, :], own_sem.at[8]),
     ]
     for copy in mine[1:]:
         copy.start()
 
-    for copy in loads[5:]:
+    for copy in loads[6:8]:
         copy.wait()
-    for copy in sibling_copies(False):
-        copy.wait_recv()
-    for dx in range(1, NX):
-
-        @pl.when(x >= dx)
-        def _():
-            for dc in range(NC):
-                for copy in x_copies(dx, dc, False):
-                    copy.wait_recv()
-            for copy in forward(dx, False):
-                copy.wait_recv()
-
+    own_kv.wait()
     for copy in swaps:
         copy.wait()
 
-    def rk_copy(hh, dx, sending):
+    def rk_copy(hh, dx, part, sending):
         px = x - dx if sending else x + dx
-        at = rows((px if sending else x) * OWN, OWN, 256)
-        return remote(
-            dks.at[hh, at, :], rxk.at[dx - 1, hh], rk_send.at[hh, dx - 1], rk_recv.at[hh, dx - 1],
-            device(y, z_lo, px, z_hi, core),
+        chunk = (px if sending else x) * NZH + (1 - z_hi if part == 0 else z_hi)
+        return remote(
+            dks.at[hh, rows(chunk * CHUNK, CHUNK, 128), :], rxk.at[dx - 1, hh, part],
+            rk_send.at[hh, part, dx - 1], rk_recv.at[hh, part, dx - 1], device(y, z_lo, px, z_hi, core),
         )
 
     def rv_copy(dx, sending):
@@ -394,58 +403,49 @@
 
     @pl.loop(0, 2)
     def _(hh):
+        sibling_copy(hh, False).wait_recv()
         for n in range(NX):
 
             @pl.when(x == n)
             def _():
                 keys, below = (n + 1) * OWN, n * OWN
-                long_head(keys, hh, z_hi, qb, gb, kb, vb, dq, scores, grads, low, acc_k, acc_v, kt)
+                for dx in range(1, n + 1):
+                    for dc in range(NC):
+                        near_copy(hh, dx, dc, False).wait_recv()
+                        forward(hh, dx, dc, False).wait_recv()
+                long_head(keys, hh, z_hi, qb, gb, kvb, scores, grads, probs, low, acc_k)
                 if below:
                     dks[hh, 0:below, :] = acc_k[0:below, :].astype(BF)
                 totk[hh] = acc_k[below:keys, :]
-                if below:
-                    dvs[hh, 0:below, :] = acc_v[0:below, :].astype(BF)
-                totv[hh] = acc_v[below:keys, :]
-
-        for dx in range(1, NX):
-
-            @pl.when(x >= dx)
-            def _():
-                rk_copy(hh, dx, True).start()
+
+        for part in range(2):
+            for dx in range(1, NX):
+
+                @pl.when(x >= dx)
+                def _():
+                    rk_copy(hh, dx, part, True).start()
 
         @pl.when(x == NX - 1)
         def _():
             zsk[hh] = totk[hh, theirs, :].astype(BF)
             zk_copy(hh).start()
 
-    for dx in range(1, NX):
-
-        @pl.when(x >= dx)
-        def _():
-            rv_copy(dx, True).start()
-
-    dq_copy = remote(
-        dq.at[rows(other * LONG_DEV, LONG_DEV, 64), :], gq.at[early, lanes(core * HALF_Q, HALF_Q)],
-        dq_send.at[0], dq_recv.at[0], sibling,
-    )
-    dq_copy.start()
-    mine.append(
-        pltpu.make_async_copy(dq.at[pair_rows, :], gq.at[early, lanes(core * HALF_Q, HALF_Q)], own_sem.at[8])
-    )
-    mine[-1].start()
-
     def sum_over_x(hh):
-        @pl.when(x < NX - 1)
-        def _():
+        for part in range(2):
+            at = theirs if part == 0 else ours
             for dx in range(1, NX):
 
                 @pl.when(x + dx < NX)
                 def _():
-                    rk_copy(hh, dx, False).wait_recv()
-                    totk[hh] += rxk[dx - 1, hh].astype(F32)
-
-            zsk[hh] = totk[hh, theirs, :].astype(BF)
-            zk_copy(hh).start()
+                    rk_copy(hh, dx, part, False).wait_recv()
+                    totk[hh, at, :] += rxk[dx - 1, hh, part].astype(F32)
+
+            if part == 0:
+
+                @pl.when(x < NX - 1)
+                def _():
+                    zsk[hh] = totk[hh, theirs, :].astype(BF)
+                    zk_copy(hh).start()
 
     def long_copy(hh, i, sign):
         py, pc = group_peer(i, sign)
@@ -453,6 +453,11 @@
         return remote(
             gkl.at[hh], gk.at[hh, sy, :, early, lanes(sc * HEAD, HEAD)], l_send.at[hh, i], l_recv.at[hh, i],
             device(py, z_lo, x, z_hi, pc),
+        )
+
+    def own_copy(hh):
+        return pltpu.make_async_copy(
+            gkl.at[hh], gk.at[hh, y, :, early, lanes(core * HEAD, HEAD)], own_sem.at[10 + hh]
         )
 
     def spread(hh):
@@ -462,11 +467,39 @@
         gkl[hh, 1] = both[LONG_DEV:]
         for i in range(len(group)):
             long_copy(hh, i, 1).start()
-        copy = pltpu.make_async_copy(
-            gkl.at[hh], gk.at[hh, y, :, early, lanes(core * HEAD, HEAD)], own_sem.at[9 + hh]
-        )
-        copy.start()
-        return copy
+        own_copy(hh).start()
+
+    @pl.when(x == NX - 1)
+    def _():
+        spread(0)
+
+    @pl.loop(0, 2)
+    def _(hh):
+        for n in range(NX):
+
+            @pl.when(x == n)
+            def _():
+                keys, below = (n + 1) * OWN, n * OWN
+                long_rest(keys, hh, gb, kvb, dq, probs, low, acc_v)
+                if below:
+                    dvs[hh, 0:below, :] = acc_v[0:below, :].astype(BF)
+                totv[hh] = acc_v[below:keys, :]
+
+    for dx in range(1, NX):
+
+        @pl.when(x >= dx)
+        def _():
+            rv_copy(dx, True).start()
+
+    dq_copy = remote(
+        dq.at[rows(other * LONG_DEV, LONG_DEV, 64), :], gq.at[early, lanes(core * HALF_Q, HALF_Q)],
+        dq_send.at[0], dq_recv.at[0], sibling,
+    )
+    dq_copy.start()
+    mine.append(
+        pltpu.make_async_copy(dq.at[pair_rows, :], gq.at[early, lanes(core * HALF_Q, HALF_Q)], own_sem.at[9])
+    )
+    mine[-1].start()
 
     def w_copy(hh, dx, sign):
         px = x_peer(dx, sign)
@@ -483,8 +516,8 @@
             result = term if result is None else result + term
         return result.reshape(NZH, 96, HALF_K)
 
-    def multiply(hh, own):
-        own.wait()
+    def multiply(hh):
+        own_copy(hh).wait()
         for i in range(len(group)):
             long_copy(hh, i, -1).wait_recv()
         for dx in (2, 1, 3):
@@ -559,6 +592,19 @@
             for dy in (2, 1, 3):
                 ny_copy(hh, dy, dz, 1).start()
 
+    updated = [
+        pltpu.make_async_copy(vmem, hbm, out_sem.at[i])
+        for i, (vmem, hbm) in enumerate(
+            ((new_master, master_out), (new_first, first_out), (new_second, second_out))
+        )
+    ]
+
+    def weight_copy(hh, b):
+        col = pl.ds((2 * b + hh) * 128, 128)
+        return pltpu.make_async_copy(
+            new_weight.at[:, :, col], weight_out.at[:, :, col], out_sem.at[3 + 2 * hh + b]
+        )
+
     def finish(hh):
         for dy in range(1, NY):
             for dz in range(NZL):
@@ -568,17 +614,22 @@
             for b in range(2):
                 both = jnp.concatenate([t[b * 24 : (b + 1) * 24] for t in two], axis=0)
                 new_weight[0, pair * 48 : (pair + 1) * 48, (2 * b + hh) * 128 : (2 * b + hh + 1) * 128] = both.astype(BF)
-
-    sum_over_x(0)
-    own = spread(0)
+        for b in range(2):
+            weight_copy(hh, b).start()
+
+    @pl.when(x < NX - 1)
+    def _():
+        sum_over_x(0)
+        spread(0)
+
     sum_over_x(1)
     mine[0].wait()
     mine[1].wait()
     for i in range(len(group)):
         x_copy(i, -1).wait_recv()
         short_copy(i, -1).wait_recv()
-    multiply(0, own)
-    own = spread(1)
+    multiply(0)
+    spread(1)
 
     @pl.when(x < NX - 1)
     def _():
@@ -591,7 +642,7 @@
 
     zsv[...] = totv[:, theirs, :].astype(BF)
     zv_copy.start()
-    multiply(1, own)
+    multiply(1)
     reduce_x(0)
     zv_copy.wait_recv()
     for hh in range(2):
@@ -601,62 +652,74 @@
     my_keys = lanes(core * HALF_K, HALF_K)
     v_copy = remote(gvl.at[other], gv.at[early, my_keys], v_send.at[0], v_recv.at[0], sibling)
     v_copy.start()
-    mine.append(pltpu.make_async_copy(gvl.at[core], gv.at[early, my_keys], own_sem.at[11]))
+    mine.append(pltpu.make_async_copy(gvl.at[core], gv.at[early, my_keys], own_sem.at[12]))
     mine[-1].start()
+    for copy in loads[8:]:
+        copy.wait()
     update(0)
     reduce_x(1)
     pass_on(0)
+
+    for hh in range(2):
+        sibling_copy(hh, True).wait_send()
+        for dc in range(NC):
+            partner_copy(hh, dc, True).wait_send()
+    for dx in range(1, NX):
+
+        @pl.when(x + dx < NX)
+        def _():
+            for hh in range(2):
+                for dc in range(NC):
+                    near_copy(hh, dx, dc, True).wait_send()
+                    forward(hh, dx, dc, True).wait_send()
+
+        @pl.when(x >= dx)
+        def _():
+            for hh in range(2):
+                for part in range(2):
+                    rk_copy(hh, dx, part, True).wait_send()
+            rv_copy(dx, True).wait_send()
+
+    for i in range(len(group)):
+        x_copy(i, 1).wait_send()
+        short_copy(i, 1).wait_send()
+        for hh in range(2):
+            long_copy(hh, i, 1).wait_send()
+    for hh in range(2):
+        zk_copy(hh).wait_send()
+        for dx in range(1, NX):
+            w_copy(hh, dx, 1).wait_send()
+    zv_copy.wait_send()
     update(1)
+    for copy in updated:
+        copy.start()
+    finish(0)
     pass_on(1)
-    finish(0)
-    finish(1)
-
     for copy in mine[2:]:
         copy.wait()
     v_copy.wait()
     dq_copy.wait()
-    zv_copy.wait_send()
-    for copy in sibling_copies(True):
-        copy.wait_send()
-    for dc in range(NC):
-        for copy in partner_copies(dc, True):
-            copy.wait_send()
-    for dx in range(1, NX):
-
-        @pl.when(x + dx < NX)
-        def _():
-            for dc in range(NC):
-                for copy in x_copies(dx, dc, True):
-                    copy.wait_send()
-            for copy in forward(dx, True):
-                copy.wait_send()
-
-        @pl.when(x >= dx)
-        def _():
-            for hh in range(2):
-                rk_copy(hh, dx, True).wait_send()
-            rv_copy(dx, True).wait_send()
-
-    for i in range(len(group)):
-        x_copy(i, 1).wait_send()
-        short_copy(i, 1).wait_send()
     for hh in range(2):
-        zk_copy(hh).wait_send()
-        for i in range(len(group)):
-            long_copy(hh, i, 1).wait_send()
-        for dx in range(1, NX):
-            w_copy(hh, dx, 1).wait_send()
         for dz in range(1, NZ):
             p_copy(hh, dz, 1).wait_send()
         for dz in range(1, NZL):
             nz_copy(hh, dz, 1).wait_send()
-        for dy in range(1, NY):
-            for dz in range(NZL):
-                ny_copy(hh, dy, dz, 1).wait_send()
+    for dy in range(1, NY):
+        for dz in range(NZL):
+            ny_copy(0, dy, dz, 1).wait_send()
+    for copy in updated:
+        copy.wait()
+    for b in range(2):
+        weight_copy(0, b).wait()
+    finish(1)
+    for dy in range(1, NY):
+        for dz in range(NZL):
+            ny_copy(1, dy, dz, 1).wait_send()
+    for b in range(2):
+        weight_copy(1, b).wait()
 
 
 HBM = pl.BlockSpec(memory_space=pltpu.HBM)
-VMEM = pl.BlockSpec(memory_space=pltpu.VMEM)
 DMA = pltpu.SemaphoreType.DMA
 
 
@@ -704,9 +767,13 @@
         kernel,
         name="step",
         out_shape=results,
-        in_specs=[HBM] * 5 + [VMEM] * 4,
-        out_specs=[HBM] * 2 + [VMEM] * 4,
+        in_specs=[HBM] * 9,
+        out_specs=[HBM] * 6,
         scratch_shapes=[
+            pltpu.VMEM((1, SHORT_DEV), jnp.int32),
+            *[pltpu.VMEM(tile, F32)] * 6,
+            pltpu.VMEM((1, 384, KD), BF),
+            pltpu.VMEM((NC, 2, LONG_DEV, 2 * HEAD), BF),
             pltpu.VMEM((SHORT_DEV, QD), BF),
             pltpu.VMEM((SHORT_DEV, QD), BF),
             pltpu.VMEM((SHORT_DEV, KD), BF),
@@ -718,20 +785,19 @@
             pltpu.VMEM((SHORT_DEV, KD), BF),
             pltpu.VMEM((CHUNK, HALF_Q), BF),
             pltpu.VMEM((CHUNK, HALF_Q), BF),
-            pltpu.VMEM((keys, HALF_K), BF),
-            pltpu.VMEM((keys, HALF_K), BF),
+            pltpu.VMEM((2, keys, 2 * HEAD), BF),
             pltpu.VMEM((CHUNK, HALF_Q), BF),
             pltpu.VMEM((keys, WIDE), F32),
             pltpu.VMEM((keys, WIDE), F32),
-            pltpu.VMEM((keys, WIDE), BF),
+            pltpu.VMEM((2, keys, GROUPS * HEAD), BF),
+            pltpu.VMEM((2, keys, GROUPS * HEAD), BF),
             pltpu.VMEM((keys, HEAD), F32),
             pltpu.VMEM((keys, HEAD), F32),
-            pltpu.VMEM((HEAD, keys), BF),
             pltpu.VMEM((2, keys, HEAD), BF),
             pltpu.VMEM((2, keys, HEAD), BF),
             pltpu.VMEM((2, OWN, HEAD), F32),
             pltpu.VMEM((2, OWN, HEAD), F32),
-            pltpu.VMEM((NX - 1, 2, OWN, HEAD), BF),
+            pltpu.VMEM((NX - 1, 2, NZH, CHUNK, HEAD), BF),
             pltpu.VMEM((NX - 1, 2, OWN, HEAD), BF),
             pltpu.VMEM((2, CHUNK, HEAD), BF),
             pltpu.VMEM((2, CHUNK, HEAD), BF),
@@ -748,13 +814,15 @@
             pltpu.VMEM((2, NZ, 48, 128), BF),
             pltpu.VMEM((2, NZ - 1, 48, 128), BF),
             pltpu.VMEM((2, NY * NZL, 48, 128), BF),
-            DMA((5,)),
-            DMA((12,)),
+            DMA((11,)),
+            DMA((8,)),
+            DMA((13,)),
+            DMA((7,)),
             *pairs(2),
             *pairs(2, 9),
-            *pairs(2, 3),
+            *pairs(2, 2, 3),
             *pairs(1),
-            *pairs(2, 3),
+            *pairs(2, 2, 3),
             *pairs(3),
             *pairs(2),
             *pairs(1),

time: 81.7 us -> 74.8 us (0.916)
  Pallas kernels: 80.5 us -> 73.3 us
    pallas_call x1, Pallas kernels: 78 us -> 70.8 us  [on_device(): pl.pallas_call(kernel, name='step', out_shape=results, in_specs=[HBM] * 9...]
where the time goes in v1:
time: 74.8 us; the launch traced here: 73.9 us
  Pallas kernels  73.3 us (98%)
    pallas_call x1, Pallas kernels, on_device(): pl.pallas_call(kernel, name='step', out_shape=results, in_specs=[HBM] * 9...  70.8 us
    pallas_call x1, Pallas kernels, on_device(): pl.pallas_call(store_kernel, name='store', out_shape=results, in_specs=[H...  2.51 us

profile of v1, /device:TPU:2, one launch (start us, length us, event | category | flops | bytes accessed | tf_op | source)
XLA Modules:
  0.0 73.9 jit_solution(17400256342032514306)
XLA Ops:
  0.6 70.8 %step.1 = (bf16[128,6144]{1,0:T(8,128)(2,1)}, bf16[128,512]{1,0:T(8,128)(2,1)}, f32[1,24,512]{2,1,0:T(8,128)}, f32[1,24,512]{2,1,0:T(8,128)}, f32[1,24,512]{2,1,0:T(8,128)}, /*index=5*/bf16[1,384,512]{2,1,0:T(8,128)(2,1)}) custom-call(bf16[128,6144]{1,0:T(8,128)(2,1)} %q_hbm.1, bf16[128,6144]{1,0:T(8,128)(2,1)} %g_hbm.1, bf16[128,512]{1,0:T(8,128)(2,1)} %k_hbm.1, ...), custom_call_target="tpu_custom_call" | custom-call | tf_op jit(solution)/shard_map/step/pallas_call | solution.py:766
  71.4 2.5 %store.1 = (bf16[128,6144]{1,0:T(8,128)(2,1)}, bf16[128,512]{1,0:T(8,128)(2,1)}, f32[1,24,512]{2,1,0:T(8,128)}, f32[1,24,512]{2,1,0:T(8,128)}, f32[1,24,512]{2,1,0:T(8,128)}, /*index=5*/bf16[1,384,512]{2,1,0:T(8,128)(2,1)}) custom-call(bf16[128,6144]{1,0:T(8,128)(2,1)} %get-tuple-element.12.refs_0_, bf16[128,512]{1,0:T(8,128)(2,1)} %get-tuple-element.13.refs_1_, ...), custom_call_target="tpu_custom_call" | custom-call | tf_op jit(solution)/shard_map/store/pallas_call | solution.py:845

commit v2 on v1

--- a/solution.py
+++ b/solution.py
@@ -11,7 +11,7 @@
 HEAD = 128
 GROUPS = 12
 HK = 4
-SHORT_FIRST = 3
+SHORT_FIRST = 4
 LONG_DEV = 64
 SHORT_DEV = 64
 TOK_DEV = 128
@@ -35,7 +35,7 @@
 EXP_FACTOR = FACTOR * 1.4426950408889634
 NEG = -1e30
 BF = jnp.bfloat16
-VMEM_LIMIT = 63 << 20
+VMEM_LIMIT = 58 << 20
 F32 = jnp.float32
 NT = (((1,), (1,)), ((), ()))
 TN = (((0,), (0,)), ((), ()))
@@ -107,8 +107,9 @@
     )
 
 
-WIDE = 4 * CHUNK
-STEPS = GROUPS // 4
+HEADS = 6
+WIDE = HEADS * CHUNK
+STEPS = GROUPS // HEADS
 OWN = NZH * CHUNK
 
 
@@ -120,9 +121,9 @@
     def _(p):
         col = lanes((hh * STEPS + p) * WIDE, WIDE)
         wide = lanes(p * WIDE, WIDE)
-        q4, g4 = q[:, col], g[:, col]
-        qs = jnp.concatenate([q4[:, i * HEAD : (i + 1) * HEAD] for i in range(4)], axis=0)
-        gs = jnp.concatenate([g4[:, i * HEAD : (i + 1) * HEAD] for i in range(4)], axis=0)
+        qw, gw = q[:, col], g[:, col]
+        qs = jnp.concatenate([qw[:, i * HEAD : (i + 1) * HEAD] for i in range(HEADS)], axis=0)
+        gs = jnp.concatenate([gw[:, i * HEAD : (i + 1) * HEAD] for i in range(HEADS)], axis=0)
         top = None
         for n in range(chunks):
             at = slice(n * CHUNK, (n + 1) * CHUNK)
@@ -168,7 +169,7 @@
     for p in range(STEPS):
         out = dot(kt, low[hh, 0:keys, p * WIDE : (p + 1) * WIDE]).astype(BF).T
         dq[:, lanes(hh * width + p * WIDE, WIDE)] = jnp.concatenate(
-            [out[i * CHUNK : (i + 1) * CHUNK] for i in range(4)], axis=1
+            [out[i * CHUNK : (i + 1) * CHUNK] for i in range(HEADS)], axis=1
         )
 
 
@@ -178,12 +179,12 @@
 
 def kernel(
     q_hbm, g_hbm, k_hbm, v_hbm, x_hbm, seg_hbm, master_hbm, first_hbm, second_hbm,
-    gq, gv, master_out, first_out, second_out, weight_out,
-    seg_ref, master, first, second, new_master, new_first, new_second, new_weight, kvs,
+    gq, gv, new_master, new_first, new_second, new_weight,
+    seg_ref, master, first, second, kvs,
     qs, gs, ks, vs, xs, xt, sdq, sgk, sgv,
     qb, gb, kvb, dq, scores, grads, probs, low, acc_k, acc_v, dks, dvs, totk, totv,
     rxk, rxv, zsk, zrk, zsv, zrv, gkl, gvl, xg, gk, wp, wr, wsum, zf, zp, zq, nwr,
-    load_sem, key_sem, own_sem, out_sem, q_send, q_recv, kv_send, kv_recv, fw_send, fw_recv, dq_send, dq_recv,
+    load_sem, key_sem, own_sem, q_send, q_recv, kv_send, kv_recv, fw_send, fw_recv, dq_send, dq_recv,
     rk_send, rk_recv, rv_send, rv_recv, zk_send, zk_recv, zv_send, zv_recv, x_send, x_recv,
     s_send, s_recv, l_send, l_recv, v_send, v_recv, w_send, w_recv, p_send, p_recv,
     nz_send, nz_recv, ny_send, ny_recv,
@@ -255,6 +256,50 @@
     for peer in peers:
         pl.semaphore_signal(barrier, inc=1, device_id=peer, device_id_type=MESH)
 
+    for copy in keyed:
+        copy.wait()
+    own_kv = pltpu.make_async_copy(kvs.at[core], kvb.at[:, own_rows, :], own_sem.at[4])
+    own_kv.start()
+    pl.semaphore_wait(barrier, len(peers))
+
+    def kv_copy(hh, px, pz, pc, slot, sending):
+        where = own_rows if sending else rows(((px * NZH + pz) * NC + pc) * LONG_DEV, LONG_DEV, 64)
+        return remote(
+            kvs.at[pc if sending else core, hh], kvb.at[hh, where, :], kv_send.at[hh, slot], kv_recv.at[hh, slot],
+            device(y, z_lo, px, pz, pc),
+        )
+
+    def partner_copy(hh, dc, sending):
+        return kv_copy(hh, x, 1 - z_hi, (core + dc) % NC, dc, sending)
+
+    def sibling_copy(hh, sending):
+        return kv_copy(hh, x, z_hi, other, 2, sending)
+
+    def near_copy(hh, dx, dc, sending):
+        return kv_copy(hh, x + dx if sending else x - dx, z_hi, (core + dc) % NC, 1 + 2 * dx + dc, sending)
+
+    for hh in range(2):
+        for dc in range(NC):
+            partner_copy(hh, dc, True).start()
+    for hh in range(2):
+        for dx in range(1, NX):
+
+            @pl.when(x + dx < NX)
+            def _():
+                for dc in range(NC):
+                    near_copy(hh, dx, dc, True).start()
+
+        sibling_copy(hh, True).start()
+
+    swaps = [
+        remote(
+            src.at[early, lanes(other * HALF_Q, HALF_Q)], dst.at[pair_rows, :], q_send.at[n], q_recv.at[n], sibling
+        )
+        for n, (src, dst) in enumerate(((q_hbm, qb), (g_hbm, gb)))
+    ]
+    for copy in swaps:
+        copy.start()
+
     loads[0].wait()
 
     @pl.loop(0, D // 1024)
@@ -263,60 +308,6 @@
             at = i * 1024 + j * 128
             xt[rows(at, 128, 128), :] = xs[:, lanes(at, 128)].T
 
-    for copy in loads[1:6]:
-        copy.wait()
-    bias = short_mask(seg_ref)
-
-    def heads(start, stop):
-        @pl.loop(start, stop)
-        def _(kh):
-            short_head(kh, bias, qs, gs, ks, vs, sdq, sgk, sgv)
-
-    heads(0, SHORT_FIRST)
-    for copy in keyed:
-        copy.wait()
-    own_kv = pltpu.make_async_copy(kvs.at[core], kvb.at[:, own_rows, :], own_sem.at[4])
-    own_kv.start()
-    pl.semaphore_wait(barrier, len(peers))
-
-    def kv_copy(hh, px, pz, pc, slot, sending):
-        where = own_rows if sending else rows(((px * NZH + pz) * NC + pc) * LONG_DEV, LONG_DEV, 64)
-        return remote(
-            kvs.at[pc if sending else core, hh], kvb.at[hh, where, :], kv_send.at[hh, slot], kv_recv.at[hh, slot],
-            device(y, z_lo, px, pz, pc),
-        )
-
-    def partner_copy(hh, dc, sending):
-        return kv_copy(hh, x, 1 - z_hi, (core + dc) % NC, dc, sending)
-
-    def sibling_copy(hh, sending):
-        return kv_copy(hh, x, z_hi, other, 2, sending)
-
-    def near_copy(hh, dx, dc, sending):
-        return kv_copy(hh, x + dx if sending else x - dx, z_hi, (core + dc) % NC, 1 + 2 * dx + dc, sending)
-
-    for hh in range(2):
-        for dc in range(NC):
-            partner_copy(hh, dc, True).start()
-    for hh in range(2):
-        for dx in range(1, NX):
-
-            @pl.when(x + dx < NX)
-            def _():
-                for dc in range(NC):
-                    near_copy(hh, dx, dc, True).start()
-
-        sibling_copy(hh, True).start()
-
-    swaps = [
-        remote(
-            src.at[early, lanes(other * HALF_Q, HALF_Q)], dst.at[pair_rows, :], q_send.at[n], q_recv.at[n], sibling
-        )
-        for n, (src, dst) in enumerate(((q_hbm, qb), (g_hbm, gb)))
-    ]
-    for copy in swaps:
-        copy.start()
-
     def x_copy(i, sign):
         py, pc = group_peer(i, sign)
         sy, sc = (y, core) if sign > 0 else (py, pc)
@@ -334,6 +325,17 @@
         )
     ]
     mine[0].start()
+
+    for copy in loads[1:6]:
+        copy.wait()
+    bias = short_mask(seg_ref)
+
+    def heads(start, stop):
+        @pl.loop(start, stop)
+        def _(kh):
+            short_head(kh, bias, qs, gs, ks, vs, sdq, sgk, sgv)
+
+    heads(0, SHORT_FIRST)
 
     def forward(hh, dx, dc, sending):
         px = x + dx if sending else x - dx
@@ -592,19 +594,6 @@
             for dy in (2, 1, 3):
                 ny_copy(hh, dy, dz, 1).start()
 
-    updated = [
-        pltpu.make_async_copy(vmem, hbm, out_sem.at[i])
-        for i, (vmem, hbm) in enumerate(
-            ((new_master, master_out), (new_first, first_out), (new_second, second_out))
-        )
-    ]
-
-    def weight_copy(hh, b):
-        col = pl.ds((2 * b + hh) * 128, 128)
-        return pltpu.make_async_copy(
-            new_weight.at[:, :, col], weight_out.at[:, :, col], out_sem.at[3 + 2 * hh + b]
-        )
-
     def finish(hh):
         for dy in range(1, NY):
             for dz in range(NZL):
@@ -614,8 +603,6 @@
             for b in range(2):
                 both = jnp.concatenate([t[b * 24 : (b + 1) * 24] for t in two], axis=0)
                 new_weight[0, pair * 48 : (pair + 1) * 48, (2 * b + hh) * 128 : (2 * b + hh + 1) * 128] = both.astype(BF)
-        for b in range(2):
-            weight_copy(hh, b).start()
 
     @pl.when(x < NX - 1)
     def _():
@@ -691,8 +678,6 @@
             w_copy(hh, dx, 1).wait_send()
     zv_copy.wait_send()
     update(1)
-    for copy in updated:
-        copy.start()
     finish(0)
     pass_on(1)
     for copy in mine[2:]:
@@ -707,19 +692,14 @@
     for dy in range(1, NY):
         for dz in range(NZL):
             ny_copy(0, dy, dz, 1).wait_send()
-    for copy in updated:
-        copy.wait()
-    for b in range(2):
-        weight_copy(0, b).wait()
     finish(1)
     for dy in range(1, NY):
         for dz in range(NZL):
             ny_copy(1, dy, dz, 1).wait_send()
-    for b in range(2):
-        weight_copy(1, b).wait()
 
 
 HBM = pl.BlockSpec(memory_space=pltpu.HBM)
+VMEM = pl.BlockSpec(memory_space=pltpu.VMEM)
 DMA = pltpu.SemaphoreType.DMA
 
 
@@ -727,25 +707,11 @@
     return jax.ShapeDtypeStruct(shape, dtype)
 
 
-STORE_CUTS = 4
-
-
 def store_kernel(*refs):
-    sources, targets, held, (sem_in, sem_out) = refs[:6], refs[6:12], refs[12:18], refs[18:]
-    cut = TOK_DEV // STORE_CUTS
-    parts = [(0, pl.ds(i * cut, cut)) for i in range(STORE_CUTS)] + [(i, pl.ds(0, n)) for i, n in ((1, TOK_DEV), (2, 1), (3, 1), (4, 1), (5, 1))]
-    loads = [
-        pltpu.make_async_copy(sources[i].at[at], held[i].at[at], sem_in.at[n]) for n, (i, at) in enumerate(parts)
-    ]
-    stores = [
-        pltpu.make_async_copy(held[i].at[at], targets[i].at[at], sem_out.at[n]) for n, (i, at) in enumerate(parts)
-    ]
-    for copy in loads:
+    copies = [pltpu.make_async_copy(refs[i], refs[6 + i], refs[12].at[i]) for i in range(6)]
+    for copy in copies:
         copy.start()
-    for load, store in zip(loads, stores):
-        load.wait()
-        store.start()
-    for copy in stores:
+    for copy in copies:
         copy.wait()
 
 
@@ -766,13 +732,12 @@
     made = pl.pallas_call(
         kernel,
         name="step",
-        out_shape=results,
+        out_shape=[pltpu.VMEM(r.shape, r.dtype) for r in results],
         in_specs=[HBM] * 9,
-        out_specs=[HBM] * 6,
+        out_specs=[VMEM] * 6,
         scratch_shapes=[
             pltpu.VMEM((1, SHORT_DEV), jnp.int32),
-            *[pltpu.VMEM(tile, F32)] * 6,
-            pltpu.VMEM((1, 384, KD), BF),
+            *[pltpu.VMEM(tile, F32)] * 3,
             pltpu.VMEM((NC, 2, LONG_DEV, 2 * HEAD), BF),
             pltpu.VMEM((SHORT_DEV, QD), BF),
             pltpu.VMEM((SHORT_DEV, QD), BF),
@@ -817,7 +782,6 @@
             DMA((11,)),
             DMA((8,)),
             DMA((13,)),
-            DMA((7,)),
             *pairs(2),
             *pairs(2, 9),
             *pairs(2, 2, 3),
@@ -846,11 +810,10 @@
         store_kernel,
         name="store",
         out_shape=results,
-        in_specs=[HBM] * 6,
+        in_specs=[VMEM] * 6,
         out_specs=[HBM] * 6,
-        scratch_shapes=[pltpu.VMEM(r.shape, r.dtype) for r in results]
-        + [DMA((STORE_CUTS + 5,)), DMA((STORE_CUTS + 5,))],
-        compiler_params=pltpu.CompilerParams(vmem_limit_bytes=VMEM_LIMIT),
+        scratch_shapes=[DMA((6,))],
+        compiler_params=pltpu.CompilerParams(vmem_limit_bytes=8 << 20),
     )(*made)
 
 

time: 74.8 us -> 71.8 us (0.960); the launches traced: 73.9 us -> 71.7 us
  Pallas kernels: 73.3 us -> 70.9 us
    pallas_call x2, Pallas kernels: 73.3 us -> 70.9 us  [the longest x1 69.5 us: on_device(): pl.pallas_call(kernel, name='step', out_shape=[pltpu.VMEM(r.shape, r.dtyp...]
where the time goes in v2:
time: 71.8 us; the launch traced here: 71.7 us
  Pallas kernels  70.9 us (99%)
  between operations  0.8 us (1%)
    pallas_call x1, Pallas kernels, on_device(): pl.pallas_call(kernel, name='step', out_shape=[pltpu.VMEM(r.shape, r.dtyp...  69.5 us

profile of v2, /device:TPU:2, one launch (start us, length us, event | category | flops | bytes accessed | tf_op | source)
XLA Modules:
  0.0 71.7 jit_solution(17616888541534207429)
XLA Ops:
  0.6 69.5 %step.1 = (bf16[128,6144]{1,0:T(8,128)(2,1)S(1)}, bf16[128,512]{1,0:T(8,128)(2,1)S(1)}, f32[1,24,512]{2,1,0:T(8,128)S(1)}, f32[1,24,512]{2,1,0:T(8,128)S(1)}, f3...) custom-call(bf16[128,6144]{1,0:T(8,128)(2,1)} %q_hbm.1, bf16[128,6144]{1,0:T(8,128)(2,1)} %g_hbm.1, ...), custom_call_target="tpu_custom_call" | custom-call | tf_op jit(solution)/shard_map/step/pallas_call | solution.py:732
  70.2 1.4 %store.1 = (bf16[128,6144]{1,0:T(8,128)(2,1)}, bf16[128,512]{1,0:T(8,128)(2,1)}, f32[1,24,512]{2,1,0:T(8,128)}, f32[1,24,512]{2,1,0:T(8,128)}, f32[1,24,512]{2,1,0:T(8,128)}, /*index=5*/bf16[1,384,512]{2,1,0:T(8,128)(2,1)}) custom-call(bf16[128,6144]{1,0:T(8,128)(2,1)S(1)} %get-tuple-element.12.refs_0_, bf16[128,512]{1,0:T(8,128)(2,1)S(1)} %get-tuple-element.13.refs_1_, ...), custom_call_target="tpu_custom_call" | custom-call | tf_op jit(solution)/shard_map/store/pallas_call | solution.py:809

commit v3 on v2

--- a/solution.py
+++ b/solution.py
@@ -554,11 +554,11 @@
             device(y, pz, x, z_hi, core),
         )
 
-    def ny_copy(hh, dy, dz, sign):
+    def ny_copy(hh, dy, sign):
         py = (y + sign * dy + NY) % NY
-        slot = (y if sign > 0 else py) * NZL + (z_lo - dz + NZL) % NZL
-        return remote(
-            nwr.at[hh, slot], nwr.at[hh, slot], ny_send.at[hh, dy - 1, dz], ny_recv.at[hh, dy - 1, dz],
+        slots = rows((y if sign > 0 else py) * NZL, NZL, 1)
+        return remote(
+            nwr.at[hh, slots], nwr.at[hh, slots], ny_send.at[hh, dy - 1], ny_recv.at[hh, dy - 1],
             device(py, z_lo, x, z_hi, core),
         )
 
@@ -585,38 +585,48 @@
         nwr[hh, d] = jnp.concatenate(fresh, axis=0).astype(BF)
         for dz in range(1, NZL):
             nz_copy(hh, dz, 1).start()
-        for dy in range(1, NY):
-            ny_copy(hh, dy, 0, 1).start()
 
     def pass_on(hh):
         for dz in (1, 3, 2):
             nz_copy(hh, dz, -1).wait_recv()
-            for dy in (2, 1, 3):
-                ny_copy(hh, dy, dz, 1).start()
+        for dy in (2, 1, 3):
+            ny_copy(hh, dy, 1).start()
 
     def finish(hh):
         for dy in range(1, NY):
-            for dz in range(NZL):
-                ny_copy(hh, dy, dz, -1).wait_recv()
+            ny_copy(hh, dy, -1).wait_recv()
         for pair in range(NY * NZL // 2):
             two = [nwr[hh, 2 * pair + i].astype(F32) for i in range(2)]
             for b in range(2):
                 both = jnp.concatenate([t[b * 24 : (b + 1) * 24] for t in two], axis=0)
                 new_weight[0, pair * 48 : (pair + 1) * 48, (2 * b + hh) * 128 : (2 * b + hh + 1) * 128] = both.astype(BF)
 
+    for hh in range(2):
+        sibling_copy(hh, True).wait_send()
+        for dc in range(NC):
+            partner_copy(hh, dc, True).wait_send()
+    for dx in range(1, NX):
+
+        @pl.when(x + dx < NX)
+        def _():
+            for hh in range(2):
+                for dc in range(NC):
+                    near_copy(hh, dx, dc, True).wait_send()
+                    forward(hh, dx, dc, True).wait_send()
+
     @pl.when(x < NX - 1)
     def _():
         sum_over_x(0)
         spread(0)
 
     sum_over_x(1)
+    spread(1)
     mine[0].wait()
     mine[1].wait()
     for i in range(len(group)):
         x_copy(i, -1).wait_recv()
         short_copy(i, -1).wait_recv()
     multiply(0)
-    spread(1)
 
     @pl.when(x < NX - 1)
     def _():
@@ -631,6 +641,10 @@
     zv_copy.start()
     multiply(1)
     reduce_x(0)
+    for copy in loads[8:]:
+        copy.wait()
+    reduce_x(1)
+    update(0)
     zv_copy.wait_recv()
     for hh in range(2):
         both = (totv[hh, ours, :] + zrv[hh].astype(F32)).astype(BF)
@@ -641,24 +655,8 @@
     v_copy.start()
     mine.append(pltpu.make_async_copy(gvl.at[core], gv.at[early, my_keys], own_sem.at[12]))
     mine[-1].start()
-    for copy in loads[8:]:
-        copy.wait()
-    update(0)
-    reduce_x(1)
-    pass_on(0)
-
-    for hh in range(2):
-        sibling_copy(hh, True).wait_send()
-        for dc in range(NC):
-            partner_copy(hh, dc, True).wait_send()
+
     for dx in range(1, NX):
-
-        @pl.when(x + dx < NX)
-        def _():
-            for hh in range(2):
-                for dc in range(NC):
-                    near_copy(hh, dx, dc, True).wait_send()
-                    forward(hh, dx, dc, True).wait_send()
 
         @pl.when(x >= dx)
         def _():
@@ -677,6 +675,7 @@
         for dx in range(1, NX):
             w_copy(hh, dx, 1).wait_send()
     zv_copy.wait_send()
+    pass_on(0)
     update(1)
     finish(0)
     pass_on(1)
@@ -690,12 +689,10 @@
         for dz in range(1, NZL):
             nz_copy(hh, dz, 1).wait_send()
     for dy in range(1, NY):
-        for dz in range(NZL):
-            ny_copy(0, dy, dz, 1).wait_send()
+        ny_copy(0, dy, 1).wait_send()
     finish(1)
     for dy in range(1, NY):
-        for dz in range(NZL):
-            ny_copy(1, dy, dz, 1).wait_send()
+        ny_copy(1, dy, 1).wait_send()
 
 
 HBM = pl.BlockSpec(memory_space=pltpu.HBM)
@@ -797,7 +794,7 @@
             *pairs(2, 3),
             *pairs(2, 7),
             *pairs(2, 3),
-            *pairs(2, 3, 4),
+            *pairs(2, 3),
         ],
         compiler_params=pltpu.CompilerParams(
             vmem_limit_bytes=VMEM_LIMIT, collective_id=1, has_side_effects=True

time: 71.8 us -> 70.3 us (0.979)
  Pallas kernels: 70.9 us -> 69.4 us
    pallas_call x1, Pallas kernels: 69.5 us -> 68 us  [on_device(): pl.pallas_call(kernel, name='step', out_shape=[pltpu.VMEM(r.shape, r.dtyp...]
where the time goes in v3:
time: 70.3 us; the launch traced here: 70.2 us
  Pallas kernels  69.4 us (99%)
  between operations  0.8 us (1%)
    pallas_call x1, Pallas kernels, on_device(): pl.pallas_call(kernel, name='step', out_shape=[pltpu.VMEM(r.shape, r.dtyp...  68 us
    pallas_call x1, Pallas kernels, on_device(): pl.pallas_call(store_kernel, name='store', out_shape=results, in_specs=[V...  1.41 us

profile of v3, /device:TPU:2, one launch (start us, length us, event | category | flops | bytes accessed | tf_op | source)
XLA Modules:
  0.0 70.2 jit_solution(3209342662559946208)
XLA Ops:
  0.6 68.0 %step.1 = (bf16[128,6144]{1,0:T(8,128)(2,1)S(1)}, bf16[128,512]{1,0:T(8,128)(2,1)S(1)}, f32[1,24,512]{2,1,0:T(8,128)S(1)}, f32[1,24,512]{2,1,0:T(8,128)S(1)}, f3...) custom-call(bf16[128,6144]{1,0:T(8,128)(2,1)} %q_hbm.1, bf16[128,6144]{1,0:T(8,128)(2,1)} %g_hbm.1, ...), custom_call_target="tpu_custom_call" | custom-call | tf_op jit(solution)/shard_map/step/pallas_call | solution.py:729
  68.6 1.4 %store.1 = (bf16[128,6144]{1,0:T(8,128)(2,1)}, bf16[128,512]{1,0:T(8,128)(2,1)}, f32[1,24,512]{2,1,0:T(8,128)}, f32[1,24,512]{2,1,0:T(8,128)}, f32[1,24,512]{2,1,0:T(8,128)}, /*index=5*/bf16[1,384,512]{2,1,0:T(8,128)(2,1)}) custom-call(bf16[128,6144]{1,0:T(8,128)(2,1)S(1)} %get-tuple-element.12.refs_0_, bf16[128,512]{1,0:T(8,128)(2,1)S(1)} %get-tuple-element.13.refs_1_, ...), custom_call_target="tpu_custom_call" | custom-call | tf_op jit(solution)/shard_map/store/pallas_call | solution.py:806

commit v4 on v3

--- a/solution.py
+++ b/solution.py
@@ -583,7 +583,7 @@
             new_master[0, :, col] = new
             fresh.append(new)
         nwr[hh, d] = jnp.concatenate(fresh, axis=0).astype(BF)
-        for dz in range(1, NZL):
+        for dz in (3, 1, 2):
             nz_copy(hh, dz, 1).start()
 
     def pass_on(hh):

time: 70.3 us -> 70.8 us (level)
  no operation moved by 1% of the time
where the time goes in v4:
time: 70.8 us; the launch traced here: 70.7 us
  Pallas kernels  69.9 us (99%)
  between operations  0.8 us (1%)
    pallas_call x1, Pallas kernels, on_device(): pl.pallas_call(kernel, name='step', out_shape=[pltpu.VMEM(r.shape, r.dtyp...  68.5 us

profile of v4, /device:TPU:2, one launch (start us, length us, event | category | flops | bytes accessed | tf_op | source)
XLA Modules:
  0.0 70.7 jit_solution(11212266077180633400)
XLA Ops:
  0.6 68.5 %step.1 = (bf16[128,6144]{1,0:T(8,128)(2,1)S(1)}, bf16[128,512]{1,0:T(8,128)(2,1)S(1)}, f32[1,24,512]{2,1,0:T(8,128)S(1)}, f32[1,24,512]{2,1,0:T(8,128)S(1)}, f3...) custom-call(bf16[128,6144]{1,0:T(8,128)(2,1)} %q_hbm.1, bf16[128,6144]{1,0:T(8,128)(2,1)} %g_hbm.1, ...), custom_call_target="tpu_custom_call" | custom-call | tf_op jit(solution)/shard_map/step/pallas_call | solution.py:729
  69.2 1.4 %store.1 = (bf16[128,6144]{1,0:T(8,128)(2,1)}, bf16[128,512]{1,0:T(8,128)(2,1)}, f32[1,24,512]{2,1,0:T(8,128)}, f32[1,24,512]{2,1,0:T(8,128)}, f32[1,24,512]{2,1,0:T(8,128)}, /*index=5*/bf16[1,384,512]{2,1,0:T(8,128)(2,1)}) custom-call(bf16[128,6144]{1,0:T(8,128)(2,1)S(1)} %get-tuple-element.12.refs_0_, bf16[128,512]{1,0:T(8,128)(2,1)S(1)} %get-tuple-element.13.refs_1_, ...), custom_call_target="tpu_custom_call" | custom-call | tf_op jit(solution)/shard_map/store/pallas_call | solution.py:806
